TPU v7x, 32 devices: a whole 2x2x4 slice. The times are simulated.
32 devices in a mesh: grp: 2 (over y), row: 4 (over z), col: 2 (over x), rep: 2 (over core).
Axes of the slice: x: 2, y: 2, z: 4, core: 2. Of those that a mesh axis runs over, the one named last changes fastest.
Arguments:
- emb_row: bfloat16 [2048, 1280], P(('grp', 'row', 'rep'), 'col'), parts along dimension 0, may hold values from -6 to 6
- emb_col: bfloat16 [512, 1280], P(('grp', 'col'), 'row'), parts along dimension 0, may hold values from -6 to 6
- proj_row: bfloat16 [1280, 64], replicated, may hold values from -0.15625 to 0.15625
- proj_col: bfloat16 [1280, 64], replicated, may hold values from -0.15625 to 0.15625
- pair_out: bfloat16 [64, 64], replicated, may hold values from -0.75 to 0.75
- pair_bias: float32 [64], replicated, may hold values from -3 to 3
- conv_weight: bfloat16 [3, 3, 64, 64], replicated, may hold values from -0.25 to 0.25
- conv_bias: float32 [64], replicated, may hold values from -3 to 3
- target: bfloat16 [64, 2048, 256], P(None, ('grp', 'row', 'rep'), 'col'), parts along dimension 1, may hold values from -6 to 6
- kept_tiles: int32 [16, 2], P(('grp', 'row', 'rep'), 'col'), parts along dimension 0, may hold values 0 or 1
Outputs:
- cell_loss: float32 [2048, 256], P(('grp', 'row', 'rep'), 'col'), parts along dimension 0
- grad_conv: float32 [6, 3, 64, 64], P('grp'), parts along dimension 0
- grad_bias: float32 [128], P('grp'), parts along dimension 0
There are 2 independent parts, one for each index of `grp`. A program takes and returns all parts, laid end to end along the dimension named above; an argument that names none is the same for every part. Nothing has to cross between parts.
All inputs are finite; a program needn't handle non-finite values. No bound on the sum of `kept_tiles` on one device may be relied on, other than what follows from the above.
Results may differ from a plain program's by a relative error of at most 0.0025.
Values may be sent and summed in bfloat16 or wider, within the bound.
No kernel may reach another device: no remote copies, remote signals or barrier semaphores. Data moves between devices by JAX's collectives and lax.ppermute only.
A program may use at most 128 MiB of HBM per device.

v0:
```python
import functools

import jax
import jax.numpy as jnp
from jax import lax
from jax.experimental import pallas as pl
from jax.experimental.pallas import tpu as pltpu
from jax.sharding import PartitionSpec as P

REACH = 2
F32 = jnp.float32
BF16 = jnp.bfloat16


def swap(x, axis, step):
    size = lax.axis_size(axis)
    return lax.ppermute(x, axis, [(i, i ^ step) for i in range(size)])


def steps(axis):
    size, step = lax.axis_size(axis), 1
    while step < size:
        yield step
        step *= 2


def tile_kernel(
    row_ref, rhs_ref, mask_ref, out_ref, pbias_ref, weight_ref, cbias_ref, target_ref,
    loss_ref, grad_ref, hid, dif_taps, feat, near, far, bias_sum, acc, *, norm
):
    chans, width = feat.shape[1], feat.shape[2]
    cols = width // 2
    pairs = feat.shape[0]
    taps = weight_ref.shape[0]
    lane = lax.broadcasted_iota(jnp.int32, (chans, cols), 1)
    pair_out = out_ref[...]
    pbias = jnp.broadcast_to(pbias_ref[...], (chans, width))
    pbias = jnp.concatenate([pbias, pbias], axis=0)

    def features(e, carry):
        zone = jnp.where(e == 0, 0, jnp.where(e == pairs - 1, 2, 1))
        mask = mask_ref[pl.ds(zone, 1), :]
        two = row_ref[e]
        scaled = jnp.concatenate([pair_out * two[0:1], pair_out * two[1:2]], axis=0).astype(BF16)
        value = jnp.dot(scaled, rhs_ref[...], preferred_element_type=F32) + pbias
        hidden = jnp.maximum(value, 0.0) * mask
        for h in range(2):
            part = slice(h * chans, (h + 1) * chans)
            place = pl.ds(pl.multiple_of(e * width + h * cols, 128), cols)
            feat[e, :, h * cols:(h + 1) * cols] = value[part, :cols]
            own, beside = hidden[part, :cols], hidden[part, cols:]
            before = pltpu.roll(jnp.where(lane >= cols - REACH, beside, own), REACH, 1)
            after = pltpu.roll(jnp.where(lane < REACH, beside, own), cols - REACH, 1)
            hid[0:chans, place] = before.astype(BF16)
            hid[chans:2 * chans, place] = own.astype(BF16)
            hid[2 * chans:3 * chans, place] = after.astype(BF16)
        return carry

    lax.fori_loop(0, pairs, features, 0, unroll=2)

    def conv(e):
        place = pl.ds(pl.multiple_of(e * width, 128), width)
        return jnp.dot(weight_ref[...], hid[:, place], preferred_element_type=F32)

    zero = jnp.zeros((chans, width), BF16)
    for tap, e in ((0, pairs - 2), (0, pairs - 1), (1, 0), (1, pairs - 1), (2, 0), (2, 1)):
        dif_taps[tap * chans:(tap + 1) * chans, e * width:(e + 1) * width] = zero
    cbias = jnp.broadcast_to(cbias_ref[...], (chans, width))
    keep = mask_ref[3:4, :]
    bias_sum[...] = jnp.zeros_like(bias_sum)
    first, second = conv(0), conv(1)
    near[...] = first[0:chans] + second[chans:2 * chans]
    far[...] = second[0:chans]

    def differences(e, carry):
        m = e - 2
        part = conv(e)
        out = near[...] + part[2 * chans:]
        near[...] = far[...] + part[chans:2 * chans]
        far[...] = part[0:chans]
        target = jnp.concatenate([target_ref[2 * m], target_ref[2 * m + 1]], axis=1).astype(F32)
        differ = keep * (feat[e - 1] + (out + cbias) - target)
        loss = 0.5 * jnp.sum(differ * differ, axis=0, keepdims=True)
        loss_ref[pl.ds(2 * m, 1), :] = loss[:, :cols]
        loss_ref[pl.ds(2 * m + 1, 1), :] = loss[:, cols:]
        bias_sum[...] += differ
        rounded = differ.astype(BF16)
        for tap in range(3):
            place = pl.ds(pl.multiple_of((m + tap) * width, 128), width)
            dif_taps[tap * chans:(tap + 1) * chans, place] = rounded
        return carry

    lax.fori_loop(2, pairs, differences, 0, unroll=2)

    chunk = width * 6 if pairs % 6 == 0 else width
    acc[...] = jnp.zeros_like(acc)

    def gradients(s, carry):
        place = pl.ds(pl.multiple_of(s * chunk, 128), chunk)
        acc[...] += lax.dot_general(
            hid[:, place], dif_taps[:, place], (((1,), (1,)), ((), ())), preferred_element_type=F32
        )
        return carry

    lax.fori_loop(0, pairs * width // chunk, gradients, 0)
    half = taps // 2
    grad_ref[0:taps, :] = acc[:, 0:2 * chans] * norm
    last = acc[:, 2 * chans:] * norm
    grad_ref[taps:taps + half, :] = jnp.concatenate([last[:half], last[half:]], axis=1)
    sums = bias_sum[:, :cols] + bias_sum[:, cols:]
    ones = jnp.ones((8, cols), F32)
    bias = lax.dot_general(
        ones, sums, (((1,), (1,)), ((), ())), preferred_element_type=F32, precision=lax.Precision.HIGHEST
    )
    grad_ref[taps + half:, :] = jnp.zeros((grad_ref.shape[0] - taps - half, 2 * chans), F32)
    grad_ref[taps + half:taps + half + 8, 0:chans] = bias * norm


def per_device(
    emb_row, emb_col, proj_row, proj_col, pair_out, pair_bias, conv_weight, conv_bias, target, kept_tiles
):
    chans, rows, cols = target.shape
    rank = pair_out.shape[0]
    row, col, rep = lax.axis_index("row"), lax.axis_index("col"), lax.axis_index("rep")
    n_row, n_col, n_rep = lax.axis_size("row"), lax.axis_size("col"), lax.axis_size("rep")
    edge = rows // kept_tiles.shape[0]
    half = rows // 2

    share = emb_row.shape[1]
    row_part = jnp.dot(
        emb_row, lax.dynamic_slice_in_dim(proj_row, col * share, share, 0), preferred_element_type=F32
    )
    share = emb_col.shape[1]
    col_part = lax.dot_general(
        lax.dynamic_slice_in_dim(proj_col, row * share, share, 0), emb_col,
        (((0,), (1,)), ((), ())), preferred_element_type=F32,
    )
    row_part = jnp.concatenate([row_part[:half], row_part[half:]], axis=1)
    kept = jnp.broadcast_to(kept_tiles.astype(F32), (8, cols))

    send = jnp.concatenate([row_part, col_part, kept], axis=0)
    row_sum = row_part
    near_by = {}
    for k in range(1, n_col):
        got = lax.ppermute(send, "col", [(i, (i + k) % n_col) for i in range(n_col)])
        row_sum = row_sum + got[:half]
        near_by[k] = got[half:]
    left, right = near_by[1], near_by[n_col - 1]
    lane = lax.broadcasted_iota(jnp.int32, (rank, cols), 1)
    side = jnp.where(lane >= cols - REACH, left[:rank], jnp.where(lane < REACH, right[:rank], 0.0))
    lane = lax.broadcasted_iota(jnp.int32, (1, cols), 1)
    side_mask = jnp.where(
        (lane >= cols - REACH) & (col > 0), left[rank:rank + 1],
        jnp.where((lane < REACH) & (col < n_col - 1), right[rank:rank + 1], 0.0),
    )

    own = jnp.concatenate(
        [row_sum[:REACH], row_sum[half - REACH:], kept[:1], side_mask, jnp.zeros((2, cols), F32)], axis=0
    )
    other = swap(own, "rep", 1)
    edges = jnp.concatenate([jnp.where(rep == 0, own, other), jnp.where(rep == 0, other, own)], axis=0)
    col_sum = jnp.concatenate([col_part, side], axis=0)
    for step in steps("row"):
        got = swap(jnp.concatenate([col_sum, edges], axis=0), "row", step)
        col_sum = col_sum + got[:2 * rank]
        edges = jnp.concatenate([edges, got[2 * rank:]], axis=0)

    block = row * n_rep + rep

    def beside(index):
        inside = (index >= 0) & (index < n_row * n_rep)
        index = jnp.clip(index, 0, n_row * n_rep - 1)
        place = ((index // n_rep) ^ row) * n_rep + index % n_rep
        found = lax.dynamic_slice_in_dim(edges, place * 8, 8, 0)
        mask = jnp.concatenate([found[4:5], found[5:6]], axis=1)
        return found, jnp.where(inside, mask, 0.0)

    above, above_mask = beside(block - 1)
    below, below_mask = beside(block + 1)
    row_feat = jnp.concatenate(
        [above[REACH:2 * REACH, rank:], row_sum[:, :rank], row_sum[:, rank:], below[:REACH, :rank]], axis=0
    ).astype(BF16).astype(F32).reshape(half + REACH, 2, rank)
    rhs = jnp.concatenate([col_sum[:rank], col_sum[rank:]], axis=1).astype(BF16)
    own_mask = jnp.concatenate([kept[:1], side_mask], axis=1)
    all_kept = jnp.concatenate([kept[:1], kept[:1]], axis=1)
    masks = jnp.concatenate(
        [above_mask, own_mask, below_mask, all_kept, jnp.zeros((4, 2 * cols), F32)], axis=0
    )

    pairs = half + REACH
    width = 2 * cols
    taps = 3 * chans
    weight = conv_weight.transpose(0, 3, 1, 2).reshape(taps, taps)
    packed = taps + taps // 2 + 16
    cell_loss, grads = pl.pallas_call(
        functools.partial(tile_kernel, norm=1.0 / (edge * edge)),
        out_shape=(
            jax.ShapeDtypeStruct((rows, cols), F32),
            jax.ShapeDtypeStruct((packed, 2 * chans), F32),
        ),
        in_specs=[pl.BlockSpec(memory_space=pltpu.VMEM)] * 8,
        out_specs=(pl.BlockSpec(memory_space=pltpu.VMEM),) * 2,
        scratch_shapes=[
            pltpu.VMEM((taps, pairs * width), BF16),
            pltpu.VMEM((taps, pairs * width), BF16),
            pltpu.VMEM((pairs, chans, width), F32),
            pltpu.VMEM((chans, width), F32),
            pltpu.VMEM((chans, width), F32),
            pltpu.VMEM((chans, width), F32),
            pltpu.VMEM((taps, taps), F32),
        ],
        compiler_params=pltpu.CompilerParams(vmem_limit_bytes=40 * 1024 * 1024),
        name="tile",
    )(
        row_feat, rhs, masks, pair_out.astype(F32).T, pair_bias[:, None], weight,
        conv_bias[:, None], target.transpose(1, 0, 2),
    )

    piece = packed // n_rep
    mine = lax.dynamic_slice_in_dim(grads, rep * piece, piece, 0)
    total = mine + swap(lax.dynamic_slice_in_dim(grads, (1 - rep) * piece, piece, 0), "rep", 1)
    for axis in ("col", "row"):
        for step in steps(axis):
            total = total + swap(total, axis, step)
    other = swap(total, "rep", 1)
    grads = jnp.concatenate([jnp.where(rep == 0, total, other), jnp.where(rep == 0, other, total)], axis=0)
    main = grads[:taps].reshape(3, chans, 2, chans).transpose(2, 0, 1, 3)
    last = grads[taps:taps + taps // 2]
    last = jnp.concatenate([last[:, :chans], last[:, chans:]], axis=0).reshape(1, 3, chans, chans)
    grad_conv = jnp.concatenate([main, last], axis=0)
    grad_bias = grads[taps + taps // 2, :chans]
    return cell_loss, grad_conv, grad_bias


def solution(mesh):
    in_specs = (
        P(("grp", "row", "rep"), "col"),
        P(("grp", "col"), "row"),
        P(),
        P(),
        P(),
        P(),
        P(),
        P(),
        P(None, ("grp", "row", "rep"), "col"),
        P(("grp", "row", "rep"), "col"),
    )
    out_specs = (P(("grp", "row", "rep"), "col"), P("grp", None, None, None), P("grp"))
    return jax.shard_map(
        per_device, mesh=mesh, in_specs=in_specs, out_specs=out_specs, check_vma=False
    )
```

profile of v0, /device:TPU:0, one launch (start us, length us, event | category | flops | bytes accessed | tf_op | source)
XLA Modules:
  0.0 64.1 jit_solution(13155125242156726504)
XLA Ops:
  0.7 0.9 %copy-done = bf16[128,640]{1,0:T(8,128)(2,1)S(1)} copy-done((bf16[128,640]{1,0:T(8,128)(2,1)S(1)}, bf16[128,640]{1,0:T(8,128)(2,1)}, u32[]{:S(2)}) %copy-start) | copy-done | bytes 163864
  1.6 1.1 %convolution_bitcast_fusion = f32[128,64]{1,0:T(8,128)S(1)} fusion(bf16[128,640]{1,0:T(8,128)(2,1)S(1)} %copy-done, bf16[1280,64]{0,1:T(8,128)(2,1)} %param.12, s32[]{:T(128)S(6)} %select_n.107), kind=kOutput, calls=%fused_computation.1 | convolution fusion | flops 10485760 | bytes 278532 | tf_op jit(solution)/shard_map/dot_general | solution.py:130
  3.3 1.1 %fusion.2 = f32[64,128]{1,0:T(8,128)S(1)} fusion(bf16[128,320]{0,1:T(8,128)(2,1)} %param.11, bf16[1280,64]{0,1:T(8,128)(2,1)} %param.13, s32[]{:T(128)S(6)} %select_n.108), kind=kOutput, calls=%fused_computation.15 | convolution fusion | flops 5242880 | bytes 163844 | tf_op jit(solution)/shard_map/dot_general | solution.py:134
  4.6 3.0 %collective-permute-start = (f32[136,128]{1,0:T(8,128)S(1)}, f32[136,128]{1,0:T(8,128)S(1)}, u32[]{:S(2)}, u32[]{:S(2)}) collective-permute-start(f32[136,128]{1,0:T(8,128)S(1)} %maximum_maximum_fusion), channel_id=1, source_target_pairs={{0,2},{2,0},{1,3},{3,1},{4,6},{6,4},{5,7},{7,5},{8,10},{10,8},{9,1... | collective-permute-start | bytes 208904 | tf_op jit(solution)/shard_map/ppermute | solution.py:145
  7.6 2.3 %collective-permute-done = f32[136,128]{1,0:T(8,128)S(1)} collective-permute-done((f32[136,128]{1,0:T(8,128)S(1)}, f32[136,128]{1,0:T(8,128)S(1)}, u32[]{:S(2)}, u32[]{:S(2)}) %collective-permute-start) | collective-permute-done | bytes 69664 | tf_op jit(solution)/shard_map/ppermute | solution.py:145
  10.1 0.8 %copy.21 = bf16[64,64]{0,1:T(8,128)(2,1)S(1)} copy(bf16[64,64]{1,0:T(8,128)(2,1)} %param.14) | data formatting | bytes 16384 | tf_op args[4]
  10.9 0.3 collective-permute-done.1
  11.3 2.2 %collective-permute-start.2 = (f32[144,128]{1,0:T(8,128)S(1)}, f32[144,128]{1,0:T(8,128)S(1)}, u32[]{:S(2)}, u32[]{:S(2)}) collective-permute-start(f32[144,128]{1,0:T(8,128)S(1)} %pad_maximum_fusion.4), channel_id=1, source_target_pairs={{0,4},{4,0},{8,12},{12,8},{1,5},{5,1},{9,13},{13,9},{2,6},{6,2},{1... | collective-permute-start | bytes 221192 | tf_op jit(solution)/shard_map/ppermute | solution.py:17
  13.5 3.0 %copy.30 = bf16[64,128,128]{2,0,1:T(8,128)(2,1)S(1)} copy(bf16[64,128,128]{2,1,0:T(8,128)(2,1)} %param.18) | data formatting | bytes 4194304 | tf_op args[8]
  16.5 0.2 copy.22
  16.7 0.2 reshape.100.weight_ref
  17.1 2.6 %collective-permute-start.3 = (f32[160,128]{1,0:T(8,128)S(1)}, f32[160,128]{1,0:T(8,128)S(1)}, u32[]{:S(2)}, u32[]{:S(2)}) collective-permute-start(f32[160,128]{1,0:T(8,128)S(1)} %pad_maximum_fusion.3), channel_id=1, source_target_pairs={{0,8},{4,12},{8,0},{12,4},{1,9},{5,13},{9,1},{13,5},{2,10},{6,14},... | collective-permute-start | bytes 245768 | tf_op jit(solution)/shard_map/ppermute | solution.py:17
  19.8 4.1 %collective-permute-done.3 = f32[160,128]{1,0:T(8,128)S(1)} collective-permute-done((f32[160,128]{1,0:T(8,128)S(1)}, f32[160,128]{1,0:T(8,128)S(1)}, u32[]{:S(2)}, u32[]{:S(2)}) %collective-permute-start.3) | collective-permute-done | bytes 81952 | tf_op jit(solution)/shard_map/ppermute | solution.py:17
  24.2 20.7 %tile.1 = (f32[128,128]{1,0:T(8,128)}, f32[304,128]{1,0:T(8,128)S(1)}) custom-call(f32[66,2,64]{2,1,0:T(2,128)S(1)} %reshape.103.row_ref, bf16[64,256]{1,0:T(8,128)(2,1)S(1)} %pad_maximum_fusion.6.rhs_ref, f32[8,256]{1,0:T(8,128)S(1)} %concatenate.88.mask_ref, f32[64,64]{1,0:T(8,128)S(1)} %convert_bitcast_fusion.out_ref, f32[64,1]{1,0:T(8,128)S(1)} %copy.24.pbias_ref, ...), custom_call_target="tpu_custom_call" | custom-call | tf_op jit(solution)/shard_map/tile/pallas_call | solution.py:195
  44.9 1.3 %collective-permute-done.4 = f32[152,128]{1,0:T(8,128)S(1)} collective-permute-done((f32[152,128]{1,0:T(8,128)S(1)}, f32[152,128]{1,0:T(8,128)S(1)}, u32[]{:S(2)}, u32[]{:S(2)}) %collective-permute-start.4) | collective-permute-done | bytes 77856 | tf_op jit(solution)/shard_map/ppermute | solution.py:17
  46.2 1.6 %collective-permute-start.5 = (f32[152,128]{1,0:T(8,128)S(1)}, f32[152,128]{1,0:T(8,128)S(1)}, u32[]{:S(2)}, u32[]{:S(2)}) collective-permute-start(f32[152,128]{1,0:T(8,128)S(1)} %dynamic-slice_add_fusion), channel_id=1, source_target_pairs={{0,2},{2,0},{1,3},{3,1},{4,6},{6,4},{5,7},{7,5},{8,10},{10,8},{9,1... | collective-permute-start | bytes 233480 | tf_op jit(solution)/shard_map/ppermute | solution.py:17
  47.8 2.9 %collective-permute-done.5 = f32[152,128]{1,0:T(8,128)S(1)} collective-permute-done((f32[152,128]{1,0:T(8,128)S(1)}, f32[152,128]{1,0:T(8,128)S(1)}, u32[]{:S(2)}, u32[]{:S(2)}) %collective-permute-start.5) | collective-permute-done | bytes 77856 | tf_op jit(solution)/shard_map/ppermute | solution.py:17
  50.8 4.4 %collective-permute-done.6 = f32[152,128]{1,0:T(8,128)S(1)} collective-permute-done((f32[152,128]{1,0:T(8,128)S(1)}, f32[152,128]{1,0:T(8,128)S(1)}, u32[]{:S(2)}, u32[]{:S(2)}) %collective-permute-start.6) | collective-permute-done | bytes 77856 | tf_op jit(solution)/shard_map/ppermute | solution.py:17
  55.2 1.4 %collective-permute-start.7 = (f32[152,128]{1,0:T(8,128)S(1)}, f32[152,128]{1,0:T(8,128)S(1)}, u32[]{:S(2)}, u32[]{:S(2)}) collective-permute-start(f32[152,128]{1,0:T(8,128)S(1)} %add.82), channel_id=1, source_target_pairs={{0,8},{4,12},{8,0},{12,4},{1,9},{5,13},{9,1},{13,5},{2,10},{6,14},... | collective-permute-start | bytes 233480 | tf_op jit(solution)/shard_map/ppermute | solution.py:17
  56.5 4.7 %collective-permute-done.7 = f32[152,128]{1,0:T(8,128)S(1)} collective-permute-done((f32[152,128]{1,0:T(8,128)S(1)}, f32[152,128]{1,0:T(8,128)S(1)}, u32[]{:S(2)}, u32[]{:S(2)}) %collective-permute-start.7) | collective-permute-done | bytes 77856 | tf_op jit(solution)/shard_map/ppermute | solution.py:17
  61.3 1.3 %collective-permute-done.8 = f32[152,128]{1,0:T(8,128)S(1)} collective-permute-done((f32[152,128]{1,0:T(8,128)S(1)}, f32[152,128]{1,0:T(8,128)S(1)}, u32[]{:S(2)}, u32[]{:S(2)}) %collective-permute-start.8) | collective-permute-done | bytes 77856 | tf_op jit(solution)/shard_map/ppermute | solution.py:17
  62.7 0.5 slice_bitcast_fusion
  63.2 0.2 reshape.101
  63.4 0.7 %pad_maximum_fusion = f32[3,3,64,64]{3,2,1,0:T(8,128)} fusion(f32[1,3,64,64]{3,2,1,0:T(8,128)S(1)} %bitcast.21, f32[2,3,64,64]{3,2,1,0:T(8,128)S(1)} %bitcast.20), kind=kLoop, calls=%fused_computation.2 | loop fusion | flops 36864 | bytes 294912 | tf_op jit(solution)/shard_map/concatenate | solution.py:230
  (60 shorter events, 1.2 us)
Async XLA Ops:
  0.6 0.9 %copy-start = (bf16[128,640]{1,0:T(8,128)(2,1)S(1)}, bf16[128,640]{1,0:T(8,128)(2,1)}, u32[]{:S(2)}) copy-start(bf16[128,640]{1,0:T(8,128)(2,1)} %param.10) | copy-start | bytes 491524
  4.6 5.3 %collective-permute-start = (f32[136,128]{1,0:T(8,128)S(1)}, f32[136,128]{1,0:T(8,128)S(1)}, u32[]{:S(2)}, u32[]{:S(2)}) collective-permute-start(f32[136,128]{1,0:T(8,128)S(1)} %maximum_maximum_fusion), channel_id=1, source_target_pairs={{0,2},{2,0},{1,3},{3,1},{4,6},{6,4},{5,7},{7,5},{8,10},{10,8},{9,1... | collective-permute-start | bytes 208904 | tf_op jit(solution)/shard_map/ppermute | solution.py:145
  10.0 1.2 %collective-permute-start.1 = (f32[8,128]{1,0:T(8,128)S(1)}, f32[8,128]{1,0:T(8,128)S(1)}, u32[]{:S(2)}, u32[]{:S(2)}) collective-permute-start(f32[8,128]{1,0:T(8,128)S(1)} %concatenate.77), channel_id=1, source_target_pairs={{0,1},{1,0},{2,3},{3,2},{4,5},{5,4},{6,7},{7,6},{8,9},{9,8},{10,11... | collective-permute-start | bytes 12296 | tf_op jit(solution)/shard_map/ppermute | solution.py:17
  11.3 5.8 %collective-permute-start.2 = (f32[144,128]{1,0:T(8,128)S(1)}, f32[144,128]{1,0:T(8,128)S(1)}, u32[]{:S(2)}, u32[]{:S(2)}) collective-permute-start(f32[144,128]{1,0:T(8,128)S(1)} %pad_maximum_fusion.4), channel_id=1, source_target_pairs={{0,4},{4,0},{8,12},{12,8},{1,5},{5,1},{9,13},{13,9},{2,6},{6,2},{1... | collective-permute-start | bytes 221192 | tf_op jit(solution)/shard_map/ppermute | solution.py:17
  13.4 3.1 %copy-start.1 = (bf16[3,3,64,64]{3,2,1,0:T(8,128)(2,1)S(1)}, bf16[3,3,64,64]{3,2,1,0:T(8,128)(2,1)}, u32[]{:S(2)}) copy-start(bf16[3,3,64,64]{3,2,1,0:T(8,128)(2,1)} %param.16) | copy-start | bytes 221188
  13.4 3.4 %copy-start.2 = (f32[64]{0:T(128)S(1)}, f32[64]{0:T(128)}, u32[]{:S(2)}) copy-start(f32[64]{0:T(128)} %param.15) | copy-start | bytes 772
  13.5 3.5 %copy-start.3 = (f32[64]{0:T(128)S(1)}, f32[64]{0:T(128)}, u32[]{:S(2)}) copy-start(f32[64]{0:T(128)} %param.17) | copy-start | bytes 772
  17.1 6.8 %collective-permute-start.3 = (f32[160,128]{1,0:T(8,128)S(1)}, f32[160,128]{1,0:T(8,128)S(1)}, u32[]{:S(2)}, u32[]{:S(2)}) collective-permute-start(f32[160,128]{1,0:T(8,128)S(1)} %pad_maximum_fusion.3), channel_id=1, source_target_pairs={{0,8},{4,12},{8,0},{12,4},{1,9},{5,13},{9,1},{13,5},{2,10},{6,14},... | collective-permute-start | bytes 245768 | tf_op jit(solution)/shard_map/ppermute | solution.py:17
  44.9 1.3 %collective-permute-start.4 = (f32[152,128]{1,0:T(8,128)S(1)}, f32[152,128]{1,0:T(8,128)S(1)}, u32[]{:S(2)}, u32[]{:S(2)}) collective-permute-start(f32[152,128]{1,0:T(8,128)S(1)} %constant_dynamic-slice_fusion), channel_id=1, source_target_pairs={{0,1},{1,0},{2,3},{3,2},{4,5},{5,4},{6,7},{7,6},{8,9},{9,8},{10,11... | collective-permute-start | bytes 233480 | tf_op jit(solution)/shard_map/ppermute | solution.py:17
  46.2 4.5 %collective-permute-start.5 = (f32[152,128]{1,0:T(8,128)S(1)}, f32[152,128]{1,0:T(8,128)S(1)}, u32[]{:S(2)}, u32[]{:S(2)}) collective-permute-start(f32[152,128]{1,0:T(8,128)S(1)} %dynamic-slice_add_fusion), channel_id=1, source_target_pairs={{0,2},{2,0},{1,3},{3,1},{4,6},{6,4},{5,7},{7,5},{8,10},{10,8},{9,1... | collective-permute-start | bytes 233480 | tf_op jit(solution)/shard_map/ppermute | solution.py:17
  50.7 4.5 %collective-permute-start.6 = (f32[152,128]{1,0:T(8,128)S(1)}, f32[152,128]{1,0:T(8,128)S(1)}, u32[]{:S(2)}, u32[]{:S(2)}) collective-permute-start(f32[152,128]{1,0:T(8,128)S(1)} %add.81), channel_id=1, source_target_pairs={{0,4},{4,0},{8,12},{12,8},{1,5},{5,1},{9,13},{13,9},{2,6},{6,2},{1... | collective-permute-start | bytes 233480 | tf_op jit(solution)/shard_map/ppermute | solution.py:17
  55.2 6.0 %collective-permute-start.7 = (f32[152,128]{1,0:T(8,128)S(1)}, f32[152,128]{1,0:T(8,128)S(1)}, u32[]{:S(2)}, u32[]{:S(2)}) collective-permute-start(f32[152,128]{1,0:T(8,128)S(1)} %add.82), channel_id=1, source_target_pairs={{0,8},{4,12},{8,0},{12,4},{1,9},{5,13},{9,1},{13,5},{2,10},{6,14},... | collective-permute-start | bytes 233480 | tf_op jit(solution)/shard_map/ppermute | solution.py:17
  61.2 1.3 %collective-permute-start.8 = (f32[152,128]{1,0:T(8,128)S(1)}, f32[152,128]{1,0:T(8,128)S(1)}, u32[]{:S(2)}, u32[]{:S(2)}) collective-permute-start(f32[152,128]{1,0:T(8,128)S(1)} %add.83), channel_id=1, source_target_pairs={{0,1},{1,0},{2,3},{3,2},{4,5},{5,4},{6,7},{7,6},{8,9},{9,8},{10,11... | collective-permute-start | bytes 233480 | tf_op jit(solution)/shard_map/ppermute | solution.py:17
where the time goes:
time: 64.4 us; the launch traced here: 64.1 us
  waiting for transfers between devices  21.1 us (33%)
  Pallas kernels  20.7 us (32%)
  starting transfers between devices  11 us (17%)
  local copies, waits for them, and re-layouts  6.33 us (10%)
  matrix products  2.21 us (3%)
  between operations  1.61 us (2%)
  other arithmetic  1.1 us (2%)
    pallas_call x1, Pallas kernels, per_device(): pl.pallas_call(functools.partial(tile_kernel, norm=1.0 / (edge * edge)),...  20.7 us
    ppermute x8, waiting for transfers between devices, swap(): return lax.ppermute(x, axis, [(i, i ^ step) for i in range(size)])  18.9 us
    ppermute x8, starting transfers between devices, swap(): return lax.ppermute(x, axis, [(i, i ^ step) for i in range(size)])  8 us
    unnamed x10, local copies, waits for them, and re-layouts  4.74 us
    ppermute x1, starting transfers between devices, per_device(): lax.ppermute(send, 'col', [(i, (i + k) % n_col) for i in range(n_col)])  3 us
    ppermute x1, waiting for transfers between devices, per_device(): lax.ppermute(send, 'col', [(i, (i + k) % n_col) for i in range(n_col)])  2.28 us
  transfers between devices with their start and end apart: 9, of which 8 were waited for; matrix products, arithmetic and copies ran while one was open for 7% of the time, Pallas kernels for 0%

commit v1 on v0

--- a/solution.py
+++ b/solution.py
@@ -26,7 +26,7 @@
 
 def tile_kernel(
     row_ref, rhs_ref, mask_ref, out_ref, pbias_ref, weight_ref, cbias_ref, target_ref,
-    loss_ref, grad_ref, hid, dif_taps, feat, near, far, bias_sum, acc, *, norm
+    loss_ref, grad_ref, hid, dif_taps, feat, near, far, bias_sum, *, norm
 ):
     chans, width = feat.shape[1], feat.shape[2]
     cols = width // 2
@@ -56,7 +56,7 @@
             hid[2 * chans:3 * chans, place] = after.astype(BF16)
         return carry
 
-    lax.fori_loop(0, pairs, features, 0, unroll=2)
+    lax.fori_loop(0, pairs, features, 0, unroll=pairs)
 
     def conv(e):
         place = pl.ds(pl.multiple_of(e * width, 128), width)
@@ -90,22 +90,14 @@
             dif_taps[tap * chans:(tap + 1) * chans, place] = rounded
         return carry
 
-    lax.fori_loop(2, pairs, differences, 0, unroll=2)
-
-    chunk = width * 6 if pairs % 6 == 0 else width
-    acc[...] = jnp.zeros_like(acc)
-
-    def gradients(s, carry):
-        place = pl.ds(pl.multiple_of(s * chunk, 128), chunk)
-        acc[...] += lax.dot_general(
-            hid[:, place], dif_taps[:, place], (((1,), (1,)), ((), ())), preferred_element_type=F32
-        )
-        return carry
-
-    lax.fori_loop(0, pairs * width // chunk, gradients, 0)
+    lax.fori_loop(2, pairs, differences, 0, unroll=pairs - 2)
+
+    grad = lax.dot_general(
+        hid[...], dif_taps[...], (((1,), (1,)), ((), ())), preferred_element_type=F32
+    ) * norm
     half = taps // 2
-    grad_ref[0:taps, :] = acc[:, 0:2 * chans] * norm
-    last = acc[:, 2 * chans:] * norm
+    grad_ref[0:taps, :] = grad[:, 0:2 * chans]
+    last = grad[:, 2 * chans:]
     grad_ref[taps:taps + half, :] = jnp.concatenate([last[:half], last[half:]], axis=1)
     sums = bias_sum[:, :cols] + bias_sum[:, cols:]
     ones = jnp.ones((8, cols), F32)
@@ -207,7 +199,6 @@
             pltpu.VMEM((chans, width), F32),
             pltpu.VMEM((chans, width), F32),
             pltpu.VMEM((chans, width), F32),
-            pltpu.VMEM((taps, taps), F32),
         ],
         compiler_params=pltpu.CompilerParams(vmem_limit_bytes=40 * 1024 * 1024),
         name="tile",

time: 64.4 us -> 50.2 us (0.78)
  Pallas kernels: 20.7 us -> 6.49 us
    pallas_call x1, Pallas kernels: 20.7 us -> 6.49 us  [per_device(): pl.pallas_call(functools.partial(tile_kernel, norm=1.0 / (edge * edge)),...]
  transfers between devices with their start and end apart: 9 -> 9, of which waited for: 8 -> 8; matrix products, arithmetic and copies ran while one was open for 7% -> 9% of each run, Pallas kernels for 0% -> 0%
where the time goes in v1:
time: 50.2 us; the launch traced here: 49.9 us
  waiting for transfers between devices  21.1 us (42%)
  starting transfers between devices  11 us (22%)
  Pallas kernels  6.49 us (13%)
  local copies, waits for them, and re-layouts  6.33 us (13%)
  matrix products  2.21 us (4%)
  between operations  1.61 us (3%)
  other arithmetic  1.1 us (2%)
    ppermute x8, waiting for transfers between devices, swap(): return lax.ppermute(x, axis, [(i, i ^ step) for i in range(size)])  18.9 us
    ppermute x8, starting transfers between devices, swap(): return lax.ppermute(x, axis, [(i, i ^ step) for i in range(size)])  8.01 us
    pallas_call x1, Pallas kernels, per_device(): pl.pallas_call(functools.partial(tile_kernel, norm=1.0 / (edge * edge)),...  6.49 us
    unnamed x10, local copies, waits for them, and re-layouts  4.74 us
    ppermute x1, starting transfers between devices, per_device(): lax.ppermute(send, 'col', [(i, (i + k) % n_col) for i in range(n_col)])  3 us
    ppermute x1, waiting for transfers between devices, per_device(): lax.ppermute(send, 'col', [(i, (i + k) % n_col) for i in range(n_col)])  2.28 us
    dot_general x1, matrix products, per_device(): lax.dot_general(lax.dynamic_slice_in_dim(proj_col, row * share, share, 0)...  1.14 us
    dot_general x1, matrix products, per_device(): jnp.dot(emb_row, lax.dynamic_slice_in_dim(proj_row, col * share, share, 0...  1.07 us
  transfers between devices with their start and end apart: 9, of which 8 were waited for; matrix products, arithmetic and copies ran while one was open for 9% of the time, Pallas kernels for 0%

profile of v1, /device:TPU:0, one launch (start us, length us, event | category | flops | bytes accessed | tf_op | source)
XLA Modules:
  0.0 49.9 jit_solution(3757920833038034647)
XLA Ops:
  0.7 0.9 %copy-done = bf16[128,640]{1,0:T(8,128)(2,1)S(1)} copy-done((bf16[128,640]{1,0:T(8,128)(2,1)S(1)}, bf16[128,640]{1,0:T(8,128)(2,1)}, u32[]{:S(2)}) %copy-start) | copy-done | bytes 163864
  1.6 1.1 %convolution_bitcast_fusion = f32[128,64]{1,0:T(8,128)S(1)} fusion(bf16[128,640]{1,0:T(8,128)(2,1)S(1)} %copy-done, bf16[1280,64]{0,1:T(8,128)(2,1)} %param.12, s32[]{:T(128)S(6)} %select_n.107), kind=kOutput, calls=%fused_computation.1 | convolution fusion | flops 10485760 | bytes 278532 | tf_op jit(solution)/shard_map/dot_general | solution.py:122
  3.3 1.1 %fusion.2 = f32[64,128]{1,0:T(8,128)S(1)} fusion(bf16[128,320]{0,1:T(8,128)(2,1)} %param.11, bf16[1280,64]{0,1:T(8,128)(2,1)} %param.13, s32[]{:T(128)S(6)} %select_n.108), kind=kOutput, calls=%fused_computation.15 | convolution fusion | flops 5242880 | bytes 163844 | tf_op jit(solution)/shard_map/dot_general | solution.py:126
  4.6 3.0 %collective-permute-start = (f32[136,128]{1,0:T(8,128)S(1)}, f32[136,128]{1,0:T(8,128)S(1)}, u32[]{:S(2)}, u32[]{:S(2)}) collective-permute-start(f32[136,128]{1,0:T(8,128)S(1)} %maximum_maximum_fusion), channel_id=1, source_target_pairs={{0,2},{2,0},{1,3},{3,1},{4,6},{6,4},{5,7},{7,5},{8,10},{10,8},{9,1... | collective-permute-start | bytes 208904 | tf_op jit(solution)/shard_map/ppermute | solution.py:137
  7.6 2.3 %collective-permute-done = f32[136,128]{1,0:T(8,128)S(1)} collective-permute-done((f32[136,128]{1,0:T(8,128)S(1)}, f32[136,128]{1,0:T(8,128)S(1)}, u32[]{:S(2)}, u32[]{:S(2)}) %collective-permute-start) | collective-permute-done | bytes 69664 | tf_op jit(solution)/shard_map/ppermute | solution.py:137
  10.1 0.8 %copy.21 = bf16[64,64]{0,1:T(8,128)(2,1)S(1)} copy(bf16[64,64]{1,0:T(8,128)(2,1)} %param.14) | data formatting | bytes 16384 | tf_op args[4]
  10.9 0.3 collective-permute-done.1
  11.3 2.2 %collective-permute-start.2 = (f32[144,128]{1,0:T(8,128)S(1)}, f32[144,128]{1,0:T(8,128)S(1)}, u32[]{:S(2)}, u32[]{:S(2)}) collective-permute-start(f32[144,128]{1,0:T(8,128)S(1)} %pad_maximum_fusion.4), channel_id=1, source_target_pairs={{0,4},{4,0},{8,12},{12,8},{1,5},{5,1},{9,13},{13,9},{2,6},{6,2},{1... | collective-permute-start | bytes 221192 | tf_op jit(solution)/shard_map/ppermute | solution.py:17
  13.5 3.0 %copy.30 = bf16[64,128,128]{2,0,1:T(8,128)(2,1)S(1)} copy(bf16[64,128,128]{2,1,0:T(8,128)(2,1)} %param.18) | data formatting | bytes 4194304 | tf_op args[8]
  16.5 0.2 copy.22
  16.7 0.2 reshape.100.weight_ref
  17.1 2.6 %collective-permute-start.3 = (f32[160,128]{1,0:T(8,128)S(1)}, f32[160,128]{1,0:T(8,128)S(1)}, u32[]{:S(2)}, u32[]{:S(2)}) collective-permute-start(f32[160,128]{1,0:T(8,128)S(1)} %pad_maximum_fusion.3), channel_id=1, source_target_pairs={{0,8},{4,12},{8,0},{12,4},{1,9},{5,13},{9,1},{13,5},{2,10},{6,14},... | collective-permute-start | bytes 245768 | tf_op jit(solution)/shard_map/ppermute | solution.py:17
  19.8 4.1 %collective-permute-done.3 = f32[160,128]{1,0:T(8,128)S(1)} collective-permute-done((f32[160,128]{1,0:T(8,128)S(1)}, f32[160,128]{1,0:T(8,128)S(1)}, u32[]{:S(2)}, u32[]{:S(2)}) %collective-permute-start.3) | collective-permute-done | bytes 81952 | tf_op jit(solution)/shard_map/ppermute | solution.py:17
  24.2 6.5 %tile.1 = (f32[128,128]{1,0:T(8,128)}, f32[304,128]{1,0:T(8,128)S(1)}) custom-call(f32[66,2,64]{2,1,0:T(2,128)S(1)} %reshape.103.row_ref, bf16[64,256]{1,0:T(8,128)(2,1)S(1)} %pad_maximum_fusion.6.rhs_ref, f32[8,256]{1,0:T(8,128)S(1)} %concatenate.88.mask_ref, f32[64,64]{1,0:T(8,128)S(1)} %convert_bitcast_fusion.out_ref, f32[64,1]{1,0:T(8,128)S(1)} %copy.24.pbias_ref, ...), custom_call_target="tpu_custom_call" | custom-call | tf_op jit(solution)/shard_map/tile/pallas_call | solution.py:187
  30.7 1.3 %collective-permute-done.4 = f32[152,128]{1,0:T(8,128)S(1)} collective-permute-done((f32[152,128]{1,0:T(8,128)S(1)}, f32[152,128]{1,0:T(8,128)S(1)}, u32[]{:S(2)}, u32[]{:S(2)}) %collective-permute-start.4) | collective-permute-done | bytes 77856 | tf_op jit(solution)/shard_map/ppermute | solution.py:17
  31.9 1.6 %collective-permute-start.5 = (f32[152,128]{1,0:T(8,128)S(1)}, f32[152,128]{1,0:T(8,128)S(1)}, u32[]{:S(2)}, u32[]{:S(2)}) collective-permute-start(f32[152,128]{1,0:T(8,128)S(1)} %dynamic-slice_add_fusion), channel_id=1, source_target_pairs={{0,2},{2,0},{1,3},{3,1},{4,6},{6,4},{5,7},{7,5},{8,10},{10,8},{9,1... | collective-permute-start | bytes 233480 | tf_op jit(solution)/shard_map/ppermute | solution.py:17
  33.6 2.9 %collective-permute-done.5 = f32[152,128]{1,0:T(8,128)S(1)} collective-permute-done((f32[152,128]{1,0:T(8,128)S(1)}, f32[152,128]{1,0:T(8,128)S(1)}, u32[]{:S(2)}, u32[]{:S(2)}) %collective-permute-start.5) | collective-permute-done | bytes 77856 | tf_op jit(solution)/shard_map/ppermute | solution.py:17
  36.5 4.4 %collective-permute-done.6 = f32[152,128]{1,0:T(8,128)S(1)} collective-permute-done((f32[152,128]{1,0:T(8,128)S(1)}, f32[152,128]{1,0:T(8,128)S(1)}, u32[]{:S(2)}, u32[]{:S(2)}) %collective-permute-start.6) | collective-permute-done | bytes 77856 | tf_op jit(solution)/shard_map/ppermute | solution.py:17
  40.9 1.4 %collective-permute-start.7 = (f32[152,128]{1,0:T(8,128)S(1)}, f32[152,128]{1,0:T(8,128)S(1)}, u32[]{:S(2)}, u32[]{:S(2)}) collective-permute-start(f32[152,128]{1,0:T(8,128)S(1)} %add.82), channel_id=1, source_target_pairs={{0,8},{4,12},{8,0},{12,4},{1,9},{5,13},{9,1},{13,5},{2,10},{6,14},... | collective-permute-start | bytes 233480 | tf_op jit(solution)/shard_map/ppermute | solution.py:17
  42.3 4.7 %collective-permute-done.7 = f32[152,128]{1,0:T(8,128)S(1)} collective-permute-done((f32[152,128]{1,0:T(8,128)S(1)}, f32[152,128]{1,0:T(8,128)S(1)}, u32[]{:S(2)}, u32[]{:S(2)}) %collective-permute-start.7) | collective-permute-done | bytes 77856 | tf_op jit(solution)/shard_map/ppermute | solution.py:17
  47.1 1.3 %collective-permute-done.8 = f32[152,128]{1,0:T(8,128)S(1)} collective-permute-done((f32[152,128]{1,0:T(8,128)S(1)}, f32[152,128]{1,0:T(8,128)S(1)}, u32[]{:S(2)}, u32[]{:S(2)}) %collective-permute-start.8) | collective-permute-done | bytes 77856 | tf_op jit(solution)/shard_map/ppermute | solution.py:17
  48.4 0.5 %slice_bitcast_fusion = f32[64]{0:T(128)} fusion(f32[152,128]{1,0:T(8,128)S(1)} %get-tuple-element.14), kind=kLoop, calls=%fused_computation.35 | loop fusion | bytes 512 | tf_op jit(solution)/shard_map/squeeze | solution.py:222
  48.9 0.2 reshape.101
  49.1 0.7 %pad_maximum_fusion = f32[3,3,64,64]{3,2,1,0:T(8,128)} fusion(f32[1,3,64,64]{3,2,1,0:T(8,128)S(1)} %bitcast.21, f32[2,3,64,64]{3,2,1,0:T(8,128)S(1)} %bitcast.20), kind=kLoop, calls=%fused_computation.2 | loop fusion | flops 36864 | bytes 294912 | tf_op jit(solution)/shard_map/concatenate | solution.py:221
  (60 shorter events, 1.2 us)
Async XLA Ops:
  0.6 0.9 %copy-start = (bf16[128,640]{1,0:T(8,128)(2,1)S(1)}, bf16[128,640]{1,0:T(8,128)(2,1)}, u32[]{:S(2)}) copy-start(bf16[128,640]{1,0:T(8,128)(2,1)} %param.10) | copy-start | bytes 491524
  4.6 5.3 %collective-permute-start = (f32[136,128]{1,0:T(8,128)S(1)}, f32[136,128]{1,0:T(8,128)S(1)}, u32[]{:S(2)}, u32[]{:S(2)}) collective-permute-start(f32[136,128]{1,0:T(8,128)S(1)} %maximum_maximum_fusion), channel_id=1, source_target_pairs={{0,2},{2,0},{1,3},{3,1},{4,6},{6,4},{5,7},{7,5},{8,10},{10,8},{9,1... | collective-permute-start | bytes 208904 | tf_op jit(solution)/shard_map/ppermute | solution.py:137
  10.0 1.2 %collective-permute-start.1 = (f32[8,128]{1,0:T(8,128)S(1)}, f32[8,128]{1,0:T(8,128)S(1)}, u32[]{:S(2)}, u32[]{:S(2)}) collective-permute-start(f32[8,128]{1,0:T(8,128)S(1)} %concatenate.77), channel_id=1, source_target_pairs={{0,1},{1,0},{2,3},{3,2},{4,5},{5,4},{6,7},{7,6},{8,9},{9,8},{10,11... | collective-permute-start | bytes 12296 | tf_op jit(solution)/shard_map/ppermute | solution.py:17
  11.3 5.8 %collective-permute-start.2 = (f32[144,128]{1,0:T(8,128)S(1)}, f32[144,128]{1,0:T(8,128)S(1)}, u32[]{:S(2)}, u32[]{:S(2)}) collective-permute-start(f32[144,128]{1,0:T(8,128)S(1)} %pad_maximum_fusion.4), channel_id=1, source_target_pairs={{0,4},{4,0},{8,12},{12,8},{1,5},{5,1},{9,13},{13,9},{2,6},{6,2},{1... | collective-permute-start | bytes 221192 | tf_op jit(solution)/shard_map/ppermute | solution.py:17
  13.4 3.1 %copy-start.1 = (bf16[3,3,64,64]{3,2,1,0:T(8,128)(2,1)S(1)}, bf16[3,3,64,64]{3,2,1,0:T(8,128)(2,1)}, u32[]{:S(2)}) copy-start(bf16[3,3,64,64]{3,2,1,0:T(8,128)(2,1)} %param.16) | copy-start | bytes 221188
  13.4 3.4 %copy-start.2 = (f32[64]{0:T(128)S(1)}, f32[64]{0:T(128)}, u32[]{:S(2)}) copy-start(f32[64]{0:T(128)} %param.15) | copy-start | bytes 772
  13.5 3.5 %copy-start.3 = (f32[64]{0:T(128)S(1)}, f32[64]{0:T(128)}, u32[]{:S(2)}) copy-start(f32[64]{0:T(128)} %param.17) | copy-start | bytes 772
  17.1 6.8 %collective-permute-start.3 = (f32[160,128]{1,0:T(8,128)S(1)}, f32[160,128]{1,0:T(8,128)S(1)}, u32[]{:S(2)}, u32[]{:S(2)}) collective-permute-start(f32[160,128]{1,0:T(8,128)S(1)} %pad_maximum_fusion.3), channel_id=1, source_target_pairs={{0,8},{4,12},{8,0},{12,4},{1,9},{5,13},{9,1},{13,5},{2,10},{6,14},... | collective-permute-start | bytes 245768 | tf_op jit(solution)/shard_map/ppermute | solution.py:17
  30.7 1.3 %collective-permute-start.4 = (f32[152,128]{1,0:T(8,128)S(1)}, f32[152,128]{1,0:T(8,128)S(1)}, u32[]{:S(2)}, u32[]{:S(2)}) collective-permute-start(f32[152,128]{1,0:T(8,128)S(1)} %constant_dynamic-slice_fusion), channel_id=1, source_target_pairs={{0,1},{1,0},{2,3},{3,2},{4,5},{5,4},{6,7},{7,6},{8,9},{9,8},{10,11... | collective-permute-start | bytes 233480 | tf_op jit(solution)/shard_map/ppermute | solution.py:17
  31.9 4.5 %collective-permute-start.5 = (f32[152,128]{1,0:T(8,128)S(1)}, f32[152,128]{1,0:T(8,128)S(1)}, u32[]{:S(2)}, u32[]{:S(2)}) collective-permute-start(f32[152,128]{1,0:T(8,128)S(1)} %dynamic-slice_add_fusion), channel_id=1, source_target_pairs={{0,2},{2,0},{1,3},{3,1},{4,6},{6,4},{5,7},{7,5},{8,10},{10,8},{9,1... | collective-permute-start | bytes 233480 | tf_op jit(solution)/shard_map/ppermute | solution.py:17
  36.4 4.5 %collective-permute-start.6 = (f32[152,128]{1,0:T(8,128)S(1)}, f32[152,128]{1,0:T(8,128)S(1)}, u32[]{:S(2)}, u32[]{:S(2)}) collective-permute-start(f32[152,128]{1,0:T(8,128)S(1)} %add.81), channel_id=1, source_target_pairs={{0,4},{4,0},{8,12},{12,8},{1,5},{5,1},{9,13},{13,9},{2,6},{6,2},{1... | collective-permute-start | bytes 233480 | tf_op jit(solution)/shard_map/ppermute | solution.py:17
  40.9 6.0 %collective-permute-start.7 = (f32[152,128]{1,0:T(8,128)S(1)}, f32[152,128]{1,0:T(8,128)S(1)}, u32[]{:S(2)}, u32[]{:S(2)}) collective-permute-start(f32[152,128]{1,0:T(8,128)S(1)} %add.82), channel_id=1, source_target_pairs={{0,8},{4,12},{8,0},{12,4},{1,9},{5,13},{9,1},{13,5},{2,10},{6,14},... | collective-permute-start | bytes 233480 | tf_op jit(solution)/shard_map/ppermute | solution.py:17
  47.0 1.3 %collective-permute-start.8 = (f32[152,128]{1,0:T(8,128)S(1)}, f32[152,128]{1,0:T(8,128)S(1)}, u32[]{:S(2)}, u32[]{:S(2)}) collective-permute-start(f32[152,128]{1,0:T(8,128)S(1)} %add.83), channel_id=1, source_target_pairs={{0,1},{1,0},{2,3},{3,2},{4,5},{5,4},{6,7},{7,6},{8,9},{9,8},{10,11... | collective-permute-start | bytes 233480 | tf_op jit(solution)/shard_map/ppermute | solution.py:17
